TPU v7x, 512 devices: a whole 4x8x8 slice. The times are simulated.
512 devices in a mesh: dp: 32 (over x, y), tp: 16 (over z, core).
Axes of the slice: x: 4, y: 8, z: 8, core: 2. Of those that a mesh axis runs over, the one named last changes fastest.
Arguments:
- embeddings: bfloat16 [12288, 192, 256], P(('dp', 'tp')), may hold values from -6 to 6
- projection: bfloat16 [256, 16], replicated, may hold values from -0.375 to 0.375
- compress: bfloat16 [256, 4], replicated, may hold values from -0.375 to 0.375
- w_up: bfloat16 [4096, 4096], P(None, 'tp'), may hold values from -0.09375 to 0.09375
- w_down: bfloat16 [4096, 768], P('tp'), may hold values from -0.125 to 0.125
- output_norm_gain: float32 [1536], P('tp'), may hold values from 0.25 to 1.75
- out_grad: bfloat16 [12288, 1536], P('dp', 'tp'), may hold values from -6 to 6
Outputs:
- block_result: bfloat16 [12288, 1536], P('dp', 'tp')
- grad_down: float32 [4096, 768], P(('tp', 'dp'))
All inputs are finite; a program needn't handle non-finite values.
Results may differ from a plain program's by a relative error of at most 0.017.
Values may be sent and summed in bfloat16 or wider, within the bound.
No kernel may reach another device: no remote copies, remote signals or barrier semaphores. Data moves between devices by JAX's collectives and lax.ppermute only.
A program may use at most 64 MiB of HBM per device.

v0:
```python
import jax
import jax.numpy as jnp
from jax import lax
from jax.sharding import PartitionSpec as P


def split_up(x, dim, devices):
    before, after = (x.shape[:dim], x.shape[dim + 1 :])
    return jnp.moveaxis(x.reshape(*before, devices, -1, *after), dim, 0)


def summed_on_arrival(x, axis, dim):
    parts = split_up(x, dim, lax.axis_size(axis))
    arrived = lax.all_to_all(parts, axis, split_axis=0, concat_axis=0, tiled=True)
    return arrived.astype(jnp.float32).sum(axis=0)


def sent_to_all(x, axis):
    devices = lax.axis_size(axis)
    return lax.all_to_all(jnp.broadcast_to(x[None], (devices, *x.shape)), axis, 0, 0, tiled=True)


def gathered_once(x, axis):
    leaves = jax.tree.leaves(x)
    sequence = sorted(range(len(leaves)), key=lambda k: -leaves[k].size)
    width = (1, *leaves[sequence[0]].shape)[-1]
    lines = [
        jnp.pad(leaves[k].reshape(-1), (0, -leaves[k].size % width)).reshape(-1, width)
        for k in sequence
    ]
    both, at, found = (sent_to_all(jnp.concatenate(lines), axis), 0, {})
    for k, line in zip(sequence, lines):
        share = both[:, at : at + len(line)].reshape(len(both), -1)
        found[k] = share[:, : leaves[k].size].reshape(-1, *leaves[k].shape)
        at += len(line)
    numbers = iter(range(len(leaves)))
    return jax.tree.map(lambda _: found[next(numbers)], x)


def joined_by_halves(pieces, combine):
    while len(jax.tree.leaves(pieces)[0]) > 1:
        pieces = jax.vmap(combine)(
            *(jax.tree.map(lambda part: part[side::2], pieces) for side in (0, 1))
        )
    return jax.tree.map(lambda part: part[0], pieces)


def joined_all(x, axis, combine):
    pieces = gathered_once(x, axis)
    return joined_by_halves(pieces, combine)


def turned_gather(arrays, axis, dims):
    turned = [jnp.moveaxis(a, dim, 0) for a, dim in zip(arrays, dims)]
    both = jnp.concatenate([t.reshape(len(t), -1) for t in turned], axis=1)
    filled, at, done = (lax.all_gather(both, axis, axis=0, tiled=True), 0, [])
    for t, dim in zip(turned, dims):
        share = filled[:, at : at + t[0].size].reshape(-1, *t.shape[1:])
        done.append(jnp.moveaxis(share, 0, dim))
        at += t[0].size
    return tuple(done)


def chan_merge(left, right):
    count_a, mean_a, dev_a = left
    count_b, mean_b, dev_b = right
    total = count_a + count_b
    delta = mean_b - mean_a
    row_average = mean_a + delta * (count_b / total)
    dev = dev_a + dev_b + delta * delta * (count_a * count_b / total)
    return (total, row_average, dev)


def on_device(embeddings, projection, compress, w_up, w_down, output_norm_gain, out_grad):
    samples = embeddings.shape[0]
    pairs = jnp.einsum(
        "sef,fk->sek", embeddings, projection, preferred_element_type=jnp.float32
    ).astype(jnp.bfloat16)
    inter = jnp.einsum(
        "sek,sef->skf", pairs, embeddings, preferred_element_type=jnp.float32
    ).reshape(samples, -1)
    center = inter - jnp.mean(inter, axis=1, keepdims=True)
    spread = jnp.mean(center * center, axis=1, keepdims=True)
    normed = (center / jnp.sqrt(spread + 1e-05)).astype(jnp.bfloat16)
    lcb = jnp.einsum(
        "sef,fj->sje", embeddings, compress, preferred_element_type=jnp.float32
    ).reshape(samples, -1)
    hidden = jax.nn.gelu(
        jnp.dot(
            lax.all_gather(normed, "tp", axis=0, tiled=True),
            w_up,
            preferred_element_type=jnp.float32,
        ),
        approximate=True,
    ).astype(jnp.bfloat16)
    group_rows = hidden.shape[0]
    tp_count = lax.axis_size("tp")
    mlp = jnp.dot(hidden, w_down, preferred_element_type=jnp.float32)
    mlp_width = mlp.shape[1]
    full_width = mlp_width + lcb.shape[1]
    width = full_width // tp_count
    mlp_share = summed_on_arrival(mlp.astype(jnp.bfloat16), "tp", 1)
    lcb_share = lax.all_to_all(
        lcb.astype(jnp.bfloat16), "tp", split_axis=1, concat_axis=0, tiled=True
    ).astype(lcb.dtype)
    mixed_rows = jnp.concatenate([mlp_share, lcb_share], axis=1)
    own_mean = jnp.mean(mixed_rows, axis=1)
    own_dev = jnp.sum((mixed_rows - own_mean[:, None]) ** 2, axis=1)
    own_count = jnp.full((), width, jnp.float32)
    total, row_average, dev = joined_all((own_count, own_mean, own_dev), "tp", chan_merge)
    inverse_deviation = 1.0 / jnp.sqrt(dev[:, None] / total + 1e-05)
    centered_rows = (mixed_rows - row_average[:, None]) * inverse_deviation
    block_result = (centered_rows * output_norm_gain).astype(jnp.bfloat16)
    scaled_rows = out_grad.astype(jnp.float32) * output_norm_gain
    entire_scaled_rows, entire_normalized_rows = tuple(
        (
            part.astype(jnp.float32)
            for part in turned_gather(
                (scaled_rows.astype(jnp.bfloat16), centered_rows.astype(jnp.bfloat16)), "tp", (1, 1)
            )
        )
    )
    first_moment = jnp.mean(entire_scaled_rows, axis=1, keepdims=True)
    second_moment = jnp.mean(entire_scaled_rows * entire_normalized_rows, axis=1, keepdims=True)
    mixed_gradient = (
        (entire_scaled_rows - first_moment - entire_normalized_rows * second_moment)
        * inverse_deviation
    ).astype(jnp.bfloat16)
    group_mlp = mlp_width // tp_count
    mlp_grad = mixed_gradient.reshape(group_rows, tp_count, -1)[:, :, :group_mlp].reshape(
        group_rows, -1
    )
    grad_down = summed_on_arrival(
        jnp.einsum("rh,rc->hc", hidden, mlp_grad, preferred_element_type=jnp.float32).astype(
            jnp.bfloat16
        ),
        "dp",
        0,
    )
    return (block_result, grad_down)


def solution(mesh):
    return jax.shard_map(
        on_device,
        mesh=mesh,
        in_specs=(
            P(("dp", "tp"), None, None),
            P(),
            P(),
            P(None, "tp"),
            P("tp", None),
            P("tp"),
            P("dp", "tp"),
        ),
        out_specs=(P("dp", "tp"), P(("tp", "dp"), None)),
        check_vma=False,
    )
```

profile of v0, /device:TPU:8, one launch (start us, length us, event | category | flops | bytes accessed | tf_op | source)
XLA Modules:
  0.0 184.7 jit_solution(13328559922858504637)
XLA Ops:
  7.2 0.0 copy-start
  7.2 0.0 copy-start.3
  7.2 0.0 all-gather.3.cloned.1.call-start
  7.2 1.6 copy-done
  8.8 1.8 fusion.26
  10.7 0.4 multiply_reduce_fusion
  11.1 0.2 copy.26
  11.3 0.8 divide_convert_fusion
  12.1 0.0 all-gather.3.cloned.1.call-update
  12.1 0.0 copy-done.3
  12.1 0.7 fusion.6
  12.9 0.1 convert_element_type.74
  13.0 0.8 reshape.145
  13.8 10.4 %all-to-all-start.1 = ((bf16[16,2,576]{2,1,0:T(2,128)(2,1)}), bf16[16,2,576]{2,1,0:T(2,128)(2,1)S(1)}, u32[]{:S(2)}, u32[]{:S(2)}) async-start(bf16[16,2,576]{2,1,0:T(2,128)(2,1)} %reshape.145), calls=%async_computation.1 | async-start | bytes 81920 | tf_op jit(solution)/shard_map/all_to_all | solution.py:103
  24.2 37.1 %all-gather.3.cloned.1.call-done = bf16[384,4096]{1,0:T(8,128)(2,1)} async-done(((bf16[24,4096]{1,0:T(8,128)(2,1)}), bf16[384,4096]{1,0:T(8,128)(2,1)}) %all-gather.3.cloned.1.call-update) | async-done | bytes 3145744 | tf_op jit(solution)/shard_map/all_gather | solution.py:90
  61.3 0.0 copy-start.6
  61.3 3.6 %fusion.29 = f32[384,256]{1,0:T(8,128)S(1)} fusion(bf16[384,4096]{1,0:T(8,128)(2,1)} %all-gather.3.cloned.1.call-done, bf16[4096,256]{1,0:T(8,128)(2,1)} %param.10), kind=kOutput, calls=%fused_computation.71 | convolution fusion | flops 805306368 | bytes 5636096 | tf_op jit(solution)/shard_map/dot_general | solution.py:89
  64.9 0.0 copy-start.7
  64.9 0.7 copy-done.7
  65.7 0.0 copy-done.6
  65.7 0.4 convolution_convert_fusion
  66.0 0.0 copy-start.4
  66.1 0.0 copy-start.2
  66.1 0.0 copy-start.5
  66.1 1.0 copy.19
  67.1 0.0 all-to-all-done.1
  67.1 4.3 %all-to-all-start = ((bf16[16,384,48]{1,2,0:T(8,128)(2,1)}), bf16[16,384,48]{1,2,0:T(8,128)(2,1)S(1)}, u32[]{:S(2)}, u32[]{:S(2)}) async-start(bf16[16,384,48]{1,2,0:T(8,128)(2,1)} %bitcast.2), calls=%async_computation | async-start | bytes 1179648 | tf_op jit(solution)/shard_map/all_to_all | solution.py:14
  71.4 0.0 all-gather.5.cloned.1.call-start
  71.5 0.1 reshape.146
  71.6 0.1 convert_reduce_fusion.4
  71.8 0.1 reduce_sum.108
  71.9 0.1 reduce_sum.110
  72.0 0.1 copy.21
  72.1 16.6 %all-to-all-done = bf16[16,384,48]{1,2,0:T(8,128)(2,1)S(1)} async-done(((bf16[16,384,48]{1,2,0:T(8,128)(2,1)}), bf16[16,384,48]{1,2,0:T(8,128)(2,1)S(1)}, u32[]{:S(2)}, u32[]{:S(2)}) %all-to-all-start) | async-done | bytes 589856 | tf_op jit(solution)/shard_map/all_to_all | solution.py:14
  88.7 0.2 convert_reduce_fusion.1
  88.9 0.0 copy-done.4
  89.0 12.5 %all_to_all.25 = f32[16,3,384]{2,1,0:T(4,128)S(1)} all-to-all(f32[16,3,384]{2,1,0:T(4,128)S(1)} %broadcast_in_dim.2), channel_id=1, replica_groups=mesh['dp'=32,'tp'=16] {'tp'}, dimensions={0} | all-to-all | bytes 147456 | tf_op jit(solution)/shard_map/all_to_all | solution.py:20
  101.5 0.1 fusion.24
  101.7 0.1 slice_reduce_fusion
  101.8 0.1 slice.104
  101.9 0.1 slice.105
  102.0 0.1 slice.108
  102.1 0.1 slice.109
  102.2 0.1 slice.112
  102.3 0.1 slice.113
  102.4 0.6 fusion.25
  105.6 0.1 multiply_add_fusion
  105.8 0.1 multiply_add_fusion.2
  106.6 0.1 multiply_add_fusion.4
  106.8 0.0 copy-done.2
  106.8 0.0 copy-done.5
  106.8 0.7 fusion.16
  107.5 0.7 pad_maximum_fusion.1
  108.2 0.0 all-gather.5.cloned.1.call-update
  108.2 40.1 %all-gather.5.cloned.1.call-done = bf16[1536,768]{1,0:T(8,128)(2,1)} async-done(((bf16[96,768]{1,0:T(8,128)(2,1)}), bf16[1536,768]{1,0:T(8,128)(2,1)}) %all-gather.5.cloned.1.call-update) | async-done | bytes 2359312 | tf_op jit(solution)/shard_map/all_gather | solution.py:56
  148.3 0.0 copy-start.1
  148.3 2.2 %convert_reduce_fusion = (f32[384]{0:T(512)S(1)}, f32[384]{0:T(512)S(1)}) fusion(bf16[1536,768]{1,0:T(8,128)(2,1)} %all-gather.5.cloned.1.call-done), kind=kLoop, calls=%fused_computation.2 | loop fusion | flops 2948352 | bytes 2362368 | tf_op jit(solution)/shard_map/reduce_sum | solution.py:123
  150.6 0.1 copy-done.1
  150.7 0.5 fusion.2
  151.2 0.1 slice.140
  151.3 0.4 copy-done.8
  151.7 0.5 fusion.4
  152.2 25.1 %all_to_all.26 = bf16[32,8,768]{2,1,0:T(8,128)(2,1)S(1)} all-to-all(bf16[32,8,768]{2,1,0:T(8,128)(2,1)S(1)} %fusion.4), channel_id=1, replica_groups=mesh['dp'=32,'tp'=16] {'dp'}, dimensions={0} | all-to-all | bytes 786432 | tf_op jit(solution)/shard_map/all_to_all | solution.py:14
  177.2 0.7 convert_reduce_fusion.3
  (34 shorter events, 0.5 us)
Async XLA Ops:
  7.2 1.7 copy-start
  7.2 5.0 %copy-start.3 = (bf16[256,4]{0,1:T(4,128)(2,1)S(1)}, bf16[256,4]{0,1:T(4,128)(2,1)}, u32[]{:S(2)}) copy-start(bf16[256,4]{0,1:T(4,128)(2,1)} %param.9) | copy-start | bytes 6148
  7.2 54.2 %all-gather.3.cloned.1.call-start = ((), (), s32[]{:S(2)}) async-start(), calls=%async_computation.4 | async-start | bytes 3342336 | tf_op jit(solution)/shard_map/all_gather | solution.py:90
  13.8 53.3 %all-to-all-start.1 = ((bf16[16,2,576]{2,1,0:T(2,128)(2,1)}), bf16[16,2,576]{2,1,0:T(2,128)(2,1)S(1)}, u32[]{:S(2)}, u32[]{:S(2)}) async-start(bf16[16,2,576]{2,1,0:T(2,128)(2,1)} %reshape.145), calls=%async_computation.1 | async-start | bytes 81920 | tf_op jit(solution)/shard_map/all_to_all | solution.py:103
  61.3 4.3 %copy-start.6 = (bf16[256,768]{1,0:T(8,128)(2,1)S(1)}, bf16[256,768]{1,0:T(8,128)(2,1)}, u32[]{:S(2)}) copy-start(bf16[256,768]{1,0:T(8,128)(2,1)} %param.11) | copy-start | bytes 1179652
  64.9 0.7 copy-start.7
  66.0 22.9 %copy-start.4 = (f32[1,384]{1,0:T(1,128)S(1)}, f32[1,384]{1,0:T(1,128)}, u32[]{:S(2)}) copy-start(f32[1,384]{1,0:T(1,128)} %constant.29.clone.1) | copy-start | bytes 4612
  66.1 40.7 %copy-start.2 = (bf16[384,96]{0,1:T(8,128)(2,1)S(1)}, bf16[384,96]{0,1:T(8,128)(2,1)}, u32[]{:S(2)}) copy-start(bf16[384,96]{0,1:T(8,128)(2,1)} %param.13) | copy-start | bytes 221188
  66.1 40.7 %copy-start.5 = (f32[96]{0:T(128)S(1)}, f32[96]{0:T(128)}, u32[]{:S(2)}) copy-start(f32[96]{0:T(128)} %param.12) | copy-start | bytes 1156
  67.1 21.5 %all-to-all-start = ((bf16[16,384,48]{1,2,0:T(8,128)(2,1)}), bf16[16,384,48]{1,2,0:T(8,128)(2,1)S(1)}, u32[]{:S(2)}, u32[]{:S(2)}) async-start(bf16[16,384,48]{1,2,0:T(8,128)(2,1)} %bitcast.2), calls=%async_computation | async-start | bytes 1179648 | tf_op jit(solution)/shard_map/all_to_all | solution.py:14
  71.4 76.9 %all-gather.5.cloned.1.call-start = ((), (), s32[]{:S(2)}) async-start(), calls=%async_computation.5 | async-start | bytes 2506752 | tf_op jit(solution)/shard_map/all_gather | solution.py:56
  148.3 2.4 %copy-start.1 = (bf16[1536,768]{1,0:T(8,128)(2,1)S(1)}, bf16[1536,768]{1,0:T(8,128)(2,1)}, u32[]{:S(2)}) copy-start(bf16[1536,768]{1,0:T(8,128)(2,1)} %all-gather.5.cloned.1.call-done) | copy-start | bytes 7077892
  150.7 1.0 copy-start.8
Sparse Core Ops, SparseCore 0:
  12.3 49.0 all-gather.2
  108.3 39.9 all-gather.4
where the time goes:
time: 185 us
  waiting for transfers between devices  93.8 us (51%)
  blocking collectives  37.6 us (20%)
  between operations  17.6 us (10%)
  starting transfers between devices  14.8 us (8%)
  local copies, waits for them, and re-layouts  7.2 us (4%)
  matrix products  6.93 us (4%)
  other arithmetic  6.77 us (4%)
    all_gather x1, waiting for transfers between devices, turned_gather(): filled, at, done = (lax.all_gather(both, axis, axis=0, tiled=True), 0, [])  40.1 us
    all_gather x1, waiting for transfers between devices, on_device(): lax.all_gather(normed, 'tp', axis=0, tiled=True)  37.1 us
    all_to_all x1, blocking collectives, summed_on_arrival(): lax.all_to_all(parts, axis, split_axis=0, concat_axis=0, tiled=True)  25.1 us
    all_to_all x1, waiting for transfers between devices, summed_on_arrival(): lax.all_to_all(parts, axis, split_axis=0, concat_axis=0, tiled=True)  16.6 us
    all_to_all x1, blocking collectives, sent_to_all(): lax.all_to_all(jnp.broadcast_to(x[None], (devices, *x.shape)), axis, 0, 0...  12.5 us
    all_to_all x1, starting transfers between devices, on_device(): lax.all_to_all(lcb.astype(jnp.bfloat16), 'tp', split_axis=1, concat_axis=...  10.4 us
    all_to_all x1, starting transfers between devices, summed_on_arrival(): lax.all_to_all(parts, axis, split_axis=0, concat_axis=0, tiled=True)  4.3 us
    unnamed x22, local copies, waits for them, and re-layouts  4.06 us
  transfers between devices with their start and end apart: 4, of which 3 were waited for; matrix products, arithmetic and copies ran while one was open for 4% of the time, Pallas kernels for 0%

commit v1 on v0

--- a/solution.py
+++ b/solution.py
@@ -2,6 +2,27 @@
 import jax.numpy as jnp
 from jax import lax
 from jax.sharding import PartitionSpec as P
+
+
+def ring_gather(value, axis, dim):
+    size, place, rows = (lax.axis_size(axis), lax.axis_index(axis), value.shape[dim])
+    right = [(i, (i + 1) % size) for i in range(size)]
+    downward = [(i, (i - 1) % size) for i in range(size)]
+    result = jnp.zeros((*value.shape[:dim], size * rows, *value.shape[dim + 1 :]), value.dtype)
+    result = lax.dynamic_update_slice_in_dim(result, value, place * rows, axis=dim)
+    from_left = from_right = value
+    halfway = size // 2
+    for step in range(1, halfway + 1):
+        from_left = lax.ppermute(from_left, axis, right)
+        result = lax.dynamic_update_slice_in_dim(
+            result, from_left, (place - step) % size * rows, axis=dim
+        )
+        if step < size - halfway:
+            from_right = lax.ppermute(from_right, axis, downward)
+            result = lax.dynamic_update_slice_in_dim(
+                result, from_right, (place + step) % size * rows, axis=dim
+            )
+    return result
 
 
 def split_up(x, dim, devices):
@@ -86,11 +107,7 @@
         "sef,fj->sje", embeddings, compress, preferred_element_type=jnp.float32
     ).reshape(samples, -1)
     hidden = jax.nn.gelu(
-        jnp.dot(
-            lax.all_gather(normed, "tp", axis=0, tiled=True),
-            w_up,
-            preferred_element_type=jnp.float32,
-        ),
+        jnp.dot(ring_gather(normed, "tp", 0), w_up, preferred_element_type=jnp.float32),
         approximate=True,
     ).astype(jnp.bfloat16)
     group_rows = hidden.shape[0]

time: 185 us -> 200 us (1.081)
  starting transfers between devices: 14.8 us -> 37.5 us
  waiting for transfers between devices: 93.8 us -> 74.4 us
  local copies, waits for them, and re-layouts: 7.2 us -> 19.2 us
    all_gather x1 -> x0, waiting for transfers between devices: 37.1 us -> none  [on_device(): lax.all_gather(normed, 'tp', axis=0, tiled=True)]
    ppermute x0 -> x15, starting transfers between devices: none -> 26.2 us  [the longest x7 26.1 us: ring_gather(): from_right = lax.ppermute(from_right, axis, downward)]
    ppermute x0 -> x15, waiting for transfers between devices: none -> 17.4 us  [the longest x8 17.3 us: ring_gather(): from_left = lax.ppermute(from_left, axis, right)]
    dynamic_update_slice x0 -> x15, local copies, waits for them, and re-layouts: none -> 10.3 us  [the longest x8 5.5 us: ring_gather(): lax.dynamic_update_slice_in_dim(result, from_left, (place - step) % size...]
    all_to_all x1, starting transfers between devices: 10.4 us -> 4.85 us  [on_device(): lax.all_to_all(lcb.astype(jnp.bfloat16), 'tp', split_axis=1, concat_axis=...]
    all_to_all x1, starting transfers between devices: 4.3 us -> 6.34 us  [summed_on_arrival(): lax.all_to_all(parts, axis, split_axis=0, concat_axis=0, tiled=True)]
    broadcast_in_dim x0 -> x1, local copies, waits for them, and re-layouts: none -> 2 us  [ring_gather(): jnp.zeros((*value.shape[:dim], size * rows, *value.shape[dim + 1:]), valu...]
    unnamed x22 -> x24, local copies, waits for them, and re-layouts: 4.06 us -> 3.72 us
  transfers between devices with their start and end apart: 4 -> 18, of which waited for: 3 -> 9; matrix products, arithmetic and copies ran while one was open for 4% -> 8% of each run, Pallas kernels for 0% -> 0%
where the time goes in v1:
time: 200 us
  waiting for transfers between devices  74.4 us (37%)
  blocking collectives  37.6 us (19%)
  starting transfers between devices  37.5 us (19%)
  local copies, waits for them, and re-layouts  19.2 us (10%)
  between operations  17.9 us (9%)
  other arithmetic  6.76 us (3%)
  matrix products  6.3 us (3%)
    all_gather x1, waiting for transfers between devices, turned_gather(): filled, at, done = (lax.all_gather(both, axis, axis=0, tiled=True), 0, [])  40.4 us
    ppermute x7, starting transfers between devices, ring_gather(): from_right = lax.ppermute(from_right, axis, downward)  26.1 us
    all_to_all x1, blocking collectives, summed_on_arrival(): lax.all_to_all(parts, axis, split_axis=0, concat_axis=0, tiled=True)  25.1 us
    ppermute x8, waiting for transfers between devices, ring_gather(): from_left = lax.ppermute(from_left, axis, right)  17.3 us
    all_to_all x1, waiting for transfers between devices, summed_on_arrival(): lax.all_to_all(parts, axis, split_axis=0, concat_axis=0, tiled=True)  16.6 us
    all_to_all x1, blocking collectives, sent_to_all(): lax.all_to_all(jnp.broadcast_to(x[None], (devices, *x.shape)), axis, 0, 0...  12.5 us
    all_to_all x1, starting transfers between devices, summed_on_arrival(): lax.all_to_all(parts, axis, split_axis=0, concat_axis=0, tiled=True)  6.34 us
    dynamic_update_slice x8, local copies, waits for them, and re-layouts, ring_gather(): lax.dynamic_update_slice_in_dim(result, from_left, (place - step) % size...  5.5 us
  transfers between devices with their start and end apart: 18, of which 9 were waited for; matrix products, arithmetic and copies ran while one was open for 8% of the time, Pallas kernels for 0%

profile of v1, /device:TPU:8, one launch (start us, length us, event | category | flops | bytes accessed | tf_op | source)
XLA Modules:
  0.0 199.6 jit_solution(2537374468786052102)
XLA Ops:
  7.2 1.7 copy-done
  8.8 1.8 fusion.26
  10.7 0.4 multiply_reduce_fusion
  11.1 0.2 copy.26
  11.3 2.0 %broadcast_in_dim.4 = bf16[384,4096]{1,0:T(8,128)(2,1)} broadcast(bf16[]{:T(256)} %constant.109.clone.1), dimensions={} | broadcast | bytes 3145730 | tf_op jit(solution)/shard_map/broadcast_in_dim | solution.py:11
  13.3 0.8 constant_dynamic-update-slice_fusion.15
  14.1 8.5 %collective-permute-start.1 = (bf16[24,4096]{1,0:T(8,128)(2,1)S(1)}, bf16[24,4096]{1,0:T(8,128)(2,1)S(1)}, u32[]{:S(2)}, u32[]{:S(2)}) collective-permute-start(bf16[24,4096]{1,0:T(8,128)(2,1)S(1)} %get-tuple-element.19), channel_id=1, source_target_pairs={{0,15},{1,0},{2,1},{3,2},{4,3},{5,4},{6,5},{7,6},{8,7},{9,8},{10,9... | collective-permute-start | bytes 589832 | tf_op jit(solution)/shard_map/ppermute | solution.py:21
  22.6 0.7 fusion.6
  23.3 0.1 convert_element_type.74
  23.5 0.8 reshape.145
  24.3 4.8 %all-to-all-start.1 = ((bf16[16,2,576]{2,1,0:T(2,128)(2,1)}), bf16[16,2,576]{2,1,0:T(2,128)(2,1)S(1)}, u32[]{:S(2)}, u32[]{:S(2)}) async-start(bf16[16,2,576]{2,1,0:T(2,128)(2,1)} %reshape.145), calls=%async_computation.1 | async-start | bytes 81920 | tf_op jit(solution)/shard_map/all_to_all | solution.py:120
  29.4 0.1 collective-permute-start.2
  29.6 2.8 %collective-permute-start.3 = (bf16[24,4096]{1,0:T(8,128)(2,1)S(1)}, bf16[24,4096]{1,0:T(8,128)(2,1)S(1)}, u32[]{:S(2)}, u32[]{:S(2)}) collective-permute-start(bf16[24,4096]{1,0:T(8,128)(2,1)S(1)} %collective-permute-done.1), channel_id=1, source_target_pairs={{0,15},{1,0},{2,1},{3,2},{4,3},{5,4},{6,5},{7,6},{8,7},{9,8},{10,9... | collective-permute-start | bytes 589832 | tf_op jit(solution)/shard_map/ppermute | solution.py:21
  32.4 0.7 constant_dynamic-update-slice_fusion.14
  33.1 0.7 constant_dynamic-update-slice_fusion.13
  33.8 2.6 %collective-permute-done.2 = bf16[24,4096]{1,0:T(8,128)(2,1)S(1)} collective-permute-done((bf16[24,4096]{1,0:T(8,128)(2,1)S(1)}, bf16[24,4096]{1,0:T(8,128)(2,1)S(1)}, u32[]{:S(2)}, u32[]{:S(2)}) %collective-permute-start.2) | collective-permute-done | bytes 196640 | tf_op jit(solution)/shard_map/ppermute | solution.py:16
  36.3 3.0 %collective-permute-start.5 = (bf16[24,4096]{1,0:T(8,128)(2,1)S(1)}, bf16[24,4096]{1,0:T(8,128)(2,1)S(1)}, u32[]{:S(2)}, u32[]{:S(2)}) collective-permute-start(bf16[24,4096]{1,0:T(8,128)(2,1)S(1)} %collective-permute-done.3), channel_id=1, source_target_pairs={{0,15},{1,0},{2,1},{3,2},{4,3},{5,4},{6,5},{7,6},{8,7},{9,8},{10,9... | collective-permute-start | bytes 589832 | tf_op jit(solution)/shard_map/ppermute | solution.py:21
  39.3 0.7 constant_dynamic-update-slice_fusion.12
  40.0 0.7 constant_dynamic-update-slice_fusion.11
  40.7 2.0 collective-permute-done.4
  42.7 3.0 %collective-permute-start.7 = (bf16[24,4096]{1,0:T(8,128)(2,1)S(1)}, bf16[24,4096]{1,0:T(8,128)(2,1)S(1)}, u32[]{:S(2)}, u32[]{:S(2)}) collective-permute-start(bf16[24,4096]{1,0:T(8,128)(2,1)S(1)} %collective-permute-done.5), channel_id=1, source_target_pairs={{0,15},{1,0},{2,1},{3,2},{4,3},{5,4},{6,5},{7,6},{8,7},{9,8},{10,9... | collective-permute-start | bytes 589832 | tf_op jit(solution)/shard_map/ppermute | solution.py:21
  45.6 0.7 constant_dynamic-update-slice_fusion.10
  46.3 0.7 constant_dynamic-update-slice_fusion.9
  47.0 2.0 collective-permute-done.6
  49.0 3.0 %collective-permute-start.9 = (bf16[24,4096]{1,0:T(8,128)(2,1)S(1)}, bf16[24,4096]{1,0:T(8,128)(2,1)S(1)}, u32[]{:S(2)}, u32[]{:S(2)}) collective-permute-start(bf16[24,4096]{1,0:T(8,128)(2,1)S(1)} %collective-permute-done.7), channel_id=1, source_target_pairs={{0,15},{1,0},{2,1},{3,2},{4,3},{5,4},{6,5},{7,6},{8,7},{9,8},{10,9... | collective-permute-start | bytes 589832 | tf_op jit(solution)/shard_map/ppermute | solution.py:21
  51.9 0.7 constant_dynamic-update-slice_fusion.8
  52.6 0.7 constant_dynamic-update-slice_fusion.7
  53.3 2.0 collective-permute-done.8
  55.3 3.0 %collective-permute-start.11 = (bf16[24,4096]{1,0:T(8,128)(2,1)S(1)}, bf16[24,4096]{1,0:T(8,128)(2,1)S(1)}, u32[]{:S(2)}, u32[]{:S(2)}) collective-permute-start(bf16[24,4096]{1,0:T(8,128)(2,1)S(1)} %collective-permute-done.9), channel_id=1, source_target_pairs={{0,15},{1,0},{2,1},{3,2},{4,3},{5,4},{6,5},{7,6},{8,7},{9,8},{10,9... | collective-permute-start | bytes 589832 | tf_op jit(solution)/shard_map/ppermute | solution.py:21
  58.2 0.7 constant_dynamic-update-slice_fusion.6
  58.9 0.7 constant_dynamic-update-slice_fusion.5
  59.6 2.0 collective-permute-done.10
  61.6 3.0 %collective-permute-start.13 = (bf16[24,4096]{1,0:T(8,128)(2,1)S(1)}, bf16[24,4096]{1,0:T(8,128)(2,1)S(1)}, u32[]{:S(2)}, u32[]{:S(2)}) collective-permute-start(bf16[24,4096]{1,0:T(8,128)(2,1)S(1)} %collective-permute-done.11), channel_id=1, source_target_pairs={{0,15},{1,0},{2,1},{3,2},{4,3},{5,4},{6,5},{7,6},{8,7},{9,8},{10,9... | collective-permute-start | bytes 589832 | tf_op jit(solution)/shard_map/ppermute | solution.py:21
  64.5 0.7 constant_dynamic-update-slice_fusion.4
  65.2 0.7 constant_dynamic-update-slice_fusion.3
  65.9 1.9 collective-permute-done.12
  67.9 0.7 constant_dynamic-update-slice_fusion.2
  68.6 0.7 constant_dynamic-update-slice_fusion.1
  69.2 4.9 %collective-permute-done.14 = bf16[24,4096]{1,0:T(8,128)(2,1)S(1)} collective-permute-done((bf16[24,4096]{1,0:T(8,128)(2,1)S(1)}, bf16[24,4096]{1,0:T(8,128)(2,1)S(1)}, u32[]{:S(2)}, u32[]{:S(2)}) %collective-permute-start.14) | collective-permute-done | bytes 196640 | tf_op jit(solution)/shard_map/ppermute | solution.py:16
  74.2 0.7 constant_dynamic-update-slice_fusion
  74.9 2.9 %fusion.29 = f32[384,256]{1,0:T(8,128)S(1)} fusion(bf16[384,4096]{1,0:T(8,128)(2,1)} %constant_dynamic-update-slice_fusion, bf16[4096,256]{1,0:T(8,128)(2,1)S(1)} %copy-done.6), kind=kOutput, calls=%fused_computation.87 | convolution fusion | flops 805306368 | bytes 5636096 | tf_op jit(solution)/shard_map/dot_general | solution.py:110
  77.8 0.7 copy-done.8
  78.5 0.4 convolution_convert_fusion
  78.9 1.0 copy.19
  80.0 6.3 %all-to-all-start = ((bf16[16,384,48]{1,2,0:T(8,128)(2,1)}), bf16[16,384,48]{1,2,0:T(8,128)(2,1)S(1)}, u32[]{:S(2)}, u32[]{:S(2)}) async-start(bf16[16,384,48]{1,2,0:T(8,128)(2,1)} %bitcast.2), calls=%async_computation | async-start | bytes 1179648 | tf_op jit(solution)/shard_map/all_to_all | solution.py:35
  86.4 0.1 reshape.146
  86.5 0.1 convert_reduce_fusion.4
  86.9 0.1 copy.21
  87.0 16.6 %all-to-all-done = bf16[16,384,48]{1,2,0:T(8,128)(2,1)S(1)} async-done(((bf16[16,384,48]{1,2,0:T(8,128)(2,1)}), bf16[16,384,48]{1,2,0:T(8,128)(2,1)S(1)}, u32[]{:S(2)}, u32[]{:S(2)}) %all-to-all-start) | async-done | bytes 589856 | tf_op jit(solution)/shard_map/all_to_all | solution.py:35
  103.5 0.2 convert_reduce_fusion.1
  103.9 12.5 %all_to_all.25 = f32[16,3,384]{2,1,0:T(4,128)S(1)} all-to-all(f32[16,3,384]{2,1,0:T(4,128)S(1)} %broadcast_in_dim.5), channel_id=1, replica_groups=mesh['dp'=32,'tp'=16] {'tp'}, dimensions={0} | all-to-all | bytes 147456 | tf_op jit(solution)/shard_map/all_to_all | solution.py:41
  116.5 0.1 slice_reduce_fusion
  116.6 0.1 slice.104
  116.8 0.1 slice.108
  117.2 0.6 fusion.25
  121.7 0.7 fusion.16
  122.4 0.7 pad_maximum_fusion.1
  123.1 40.4 %all-gather.2.cloned.1.call-done = bf16[1536,768]{1,0:T(8,128)(2,1)} async-done(((bf16[96,768]{1,0:T(8,128)(2,1)}), bf16[1536,768]{1,0:T(8,128)(2,1)}) %all-gather.2.cloned.1.call-update) | async-done | bytes 2359312 | tf_op jit(solution)/shard_map/all_gather | solution.py:77
  163.5 2.2 %convert_reduce_fusion = (f32[384]{0:T(512)S(1)}, f32[384]{0:T(512)S(1)}) fusion(bf16[1536,768]{1,0:T(8,128)(2,1)} %all-gather.2.cloned.1.call-done), kind=kLoop, calls=%fused_computation.2 | loop fusion | flops 2948352 | bytes 2362368 | tf_op jit(solution)/shard_map/reduce_sum | solution.py:140
  165.8 0.1 copy-done.1
  165.9 0.5 fusion.2
  166.5 0.5 fusion.4
  167.0 25.1 %all_to_all.26 = bf16[32,8,768]{2,1,0:T(8,128)(2,1)S(1)} all-to-all(bf16[32,8,768]{2,1,0:T(8,128)(2,1)S(1)} %fusion.4), channel_id=1, replica_groups=mesh['dp'=32,'tp'=16] {'dp'}, dimensions={0} | all-to-all | bytes 786432 | tf_op jit(solution)/shard_map/all_to_all | solution.py:35
  192.1 0.7 convert_reduce_fusion.3
  (79 shorter events, 1.5 us)
Async XLA Ops:
  7.2 1.7 copy-start
  10.7 11.9 %copy-start.3 = (bf16[256,4]{0,1:T(4,128)(2,1)S(1)}, bf16[256,4]{0,1:T(4,128)(2,1)}, u32[]{:S(2)}) copy-start(bf16[256,4]{0,1:T(4,128)(2,1)} %param.9) | copy-start | bytes 6148
  14.1 15.3 %collective-permute-start = (bf16[24,4096]{1,0:T(8,128)(2,1)S(1)}, bf16[24,4096]{1,0:T(8,128)(2,1)S(1)}, u32[]{:S(2)}, u32[]{:S(2)}) collective-permute-start(bf16[24,4096]{1,0:T(8,128)(2,1)S(1)} %get-tuple-element.19), channel_id=1, source_target_pairs={{0,1},{1,2},{2,3},{3,4},{4,5},{5,6},{6,7},{7,8},{8,9},{9,10},{10,1... | collective-permute-start | bytes 589832 | tf_op jit(solution)/shard_map/ppermute | solution.py:16
  14.1 15.4 %collective-permute-start.1 = (bf16[24,4096]{1,0:T(8,128)(2,1)S(1)}, bf16[24,4096]{1,0:T(8,128)(2,1)S(1)}, u32[]{:S(2)}, u32[]{:S(2)}) collective-permute-start(bf16[24,4096]{1,0:T(8,128)(2,1)S(1)} %get-tuple-element.19), channel_id=1, source_target_pairs={{0,15},{1,0},{2,1},{3,2},{4,3},{5,4},{6,5},{7,6},{8,7},{9,8},{10,9... | collective-permute-start | bytes 589832 | tf_op jit(solution)/shard_map/ppermute | solution.py:21
  24.3 55.7 %all-to-all-start.1 = ((bf16[16,2,576]{2,1,0:T(2,128)(2,1)}), bf16[16,2,576]{2,1,0:T(2,128)(2,1)S(1)}, u32[]{:S(2)}, u32[]{:S(2)}) async-start(bf16[16,2,576]{2,1,0:T(2,128)(2,1)} %reshape.145), calls=%async_computation.1 | async-start | bytes 81920 | tf_op jit(solution)/shard_map/all_to_all | solution.py:120
  29.4 45.5 %copy-start.6 = (bf16[4096,256]{1,0:T(8,128)(2,1)S(1)}, bf16[4096,256]{1,0:T(8,128)(2,1)}, u32[]{:S(2)}) copy-start(bf16[4096,256]{1,0:T(8,128)(2,1)} %param.10) | copy-start | bytes 6291460
  29.4 6.9 %collective-permute-start.2 = (bf16[24,4096]{1,0:T(8,128)(2,1)S(1)}, bf16[24,4096]{1,0:T(8,128)(2,1)S(1)}, u32[]{:S(2)}, u32[]{:S(2)}) collective-permute-start(bf16[24,4096]{1,0:T(8,128)(2,1)S(1)} %collective-permute-done), channel_id=1, source_target_pairs={{0,1},{1,2},{2,3},{3,4},{4,5},{5,6},{6,7},{7,8},{8,9},{9,10},{10,1... | collective-permute-start | bytes 589832 | tf_op jit(solution)/shard_map/ppermute | solution.py:16
  29.6 6.8 %collective-permute-start.3 = (bf16[24,4096]{1,0:T(8,128)(2,1)S(1)}, bf16[24,4096]{1,0:T(8,128)(2,1)S(1)}, u32[]{:S(2)}, u32[]{:S(2)}) collective-permute-start(bf16[24,4096]{1,0:T(8,128)(2,1)S(1)} %collective-permute-done.1), channel_id=1, source_target_pairs={{0,15},{1,0},{2,1},{3,2},{4,3},{5,4},{6,5},{7,6},{8,7},{9,8},{10,9... | collective-permute-start | bytes 589832 | tf_op jit(solution)/shard_map/ppermute | solution.py:21
  36.3 6.3 %collective-permute-start.4 = (bf16[24,4096]{1,0:T(8,128)(2,1)S(1)}, bf16[24,4096]{1,0:T(8,128)(2,1)S(1)}, u32[]{:S(2)}, u32[]{:S(2)}) collective-permute-start(bf16[24,4096]{1,0:T(8,128)(2,1)S(1)} %collective-permute-done.2), channel_id=1, source_target_pairs={{0,1},{1,2},{2,3},{3,4},{4,5},{5,6},{6,7},{7,8},{8,9},{9,10},{10,1... | collective-permute-start | bytes 589832 | tf_op jit(solution)/shard_map/ppermute | solution.py:16
  36.3 6.3 %collective-permute-start.5 = (bf16[24,4096]{1,0:T(8,128)(2,1)S(1)}, bf16[24,4096]{1,0:T(8,128)(2,1)S(1)}, u32[]{:S(2)}, u32[]{:S(2)}) collective-permute-start(bf16[24,4096]{1,0:T(8,128)(2,1)S(1)} %collective-permute-done.3), channel_id=1, source_target_pairs={{0,15},{1,0},{2,1},{3,2},{4,3},{5,4},{6,5},{7,6},{8,7},{9,8},{10,9... | collective-permute-start | bytes 589832 | tf_op jit(solution)/shard_map/ppermute | solution.py:21
  42.6 6.3 %collective-permute-start.6 = (bf16[24,4096]{1,0:T(8,128)(2,1)S(1)}, bf16[24,4096]{1,0:T(8,128)(2,1)S(1)}, u32[]{:S(2)}, u32[]{:S(2)}) collective-permute-start(bf16[24,4096]{1,0:T(8,128)(2,1)S(1)} %collective-permute-done.4), channel_id=1, source_target_pairs={{0,1},{1,2},{2,3},{3,4},{4,5},{5,6},{6,7},{7,8},{8,9},{9,10},{10,1... | collective-permute-start | bytes 589832 | tf_op jit(solution)/shard_map/ppermute | solution.py:16
  42.7 6.3 %collective-permute-start.7 = (bf16[24,4096]{1,0:T(8,128)(2,1)S(1)}, bf16[24,4096]{1,0:T(8,128)(2,1)S(1)}, u32[]{:S(2)}, u32[]{:S(2)}) collective-permute-start(bf16[24,4096]{1,0:T(8,128)(2,1)S(1)} %collective-permute-done.5), channel_id=1, source_target_pairs={{0,15},{1,0},{2,1},{3,2},{4,3},{5,4},{6,5},{7,6},{8,7},{9,8},{10,9... | collective-permute-start | bytes 589832 | tf_op jit(solution)/shard_map/ppermute | solution.py:21
  49.0 6.3 %collective-permute-start.8 = (bf16[24,4096]{1,0:T(8,128)(2,1)S(1)}, bf16[24,4096]{1,0:T(8,128)(2,1)S(1)}, u32[]{:S(2)}, u32[]{:S(2)}) collective-permute-start(bf16[24,4096]{1,0:T(8,128)(2,1)S(1)} %collective-permute-done.6), channel_id=1, source_target_pairs={{0,1},{1,2},{2,3},{3,4},{4,5},{5,6},{6,7},{7,8},{8,9},{9,10},{10,1... | collective-permute-start | bytes 589832 | tf_op jit(solution)/shard_map/ppermute | solution.py:16
  49.0 6.3 %collective-permute-start.9 = (bf16[24,4096]{1,0:T(8,128)(2,1)S(1)}, bf16[24,4096]{1,0:T(8,128)(2,1)S(1)}, u32[]{:S(2)}, u32[]{:S(2)}) collective-permute-start(bf16[24,4096]{1,0:T(8,128)(2,1)S(1)} %collective-permute-done.7), channel_id=1, source_target_pairs={{0,15},{1,0},{2,1},{3,2},{4,3},{5,4},{6,5},{7,6},{8,7},{9,8},{10,9... | collective-permute-start | bytes 589832 | tf_op jit(solution)/shard_map/ppermute | solution.py:21
  55.3 6.3 %collective-permute-start.10 = (bf16[24,4096]{1,0:T(8,128)(2,1)S(1)}, bf16[24,4096]{1,0:T(8,128)(2,1)S(1)}, u32[]{:S(2)}, u32[]{:S(2)}) collective-permute-start(bf16[24,4096]{1,0:T(8,128)(2,1)S(1)} %collective-permute-done.8), channel_id=1, source_target_pairs={{0,1},{1,2},{2,3},{3,4},{4,5},{5,6},{6,7},{7,8},{8,9},{9,10},{10,1... | collective-permute-start | bytes 589832 | tf_op jit(solution)/shard_map/ppermute | solution.py:16
  55.3 6.3 %collective-permute-start.11 = (bf16[24,4096]{1,0:T(8,128)(2,1)S(1)}, bf16[24,4096]{1,0:T(8,128)(2,1)S(1)}, u32[]{:S(2)}, u32[]{:S(2)}) collective-permute-start(bf16[24,4096]{1,0:T(8,128)(2,1)S(1)} %collective-permute-done.9), channel_id=1, source_target_pairs={{0,15},{1,0},{2,1},{3,2},{4,3},{5,4},{6,5},{7,6},{8,7},{9,8},{10,9... | collective-permute-start | bytes 589832 | tf_op jit(solution)/shard_map/ppermute | solution.py:21
  61.6 6.3 %collective-permute-start.12 = (bf16[24,4096]{1,0:T(8,128)(2,1)S(1)}, bf16[24,4096]{1,0:T(8,128)(2,1)S(1)}, u32[]{:S(2)}, u32[]{:S(2)}) collective-permute-start(bf16[24,4096]{1,0:T(8,128)(2,1)S(1)} %collective-permute-done.10), channel_id=1, source_target_pairs={{0,1},{1,2},{2,3},{3,4},{4,5},{5,6},{6,7},{7,8},{8,9},{9,10},{10,1... | collective-permute-start | bytes 589832 | tf_op jit(solution)/shard_map/ppermute | solution.py:16
  61.6 7.0 %collective-permute-start.13 = (bf16[24,4096]{1,0:T(8,128)(2,1)S(1)}, bf16[24,4096]{1,0:T(8,128)(2,1)S(1)}, u32[]{:S(2)}, u32[]{:S(2)}) collective-permute-start(bf16[24,4096]{1,0:T(8,128)(2,1)S(1)} %collective-permute-done.11), channel_id=1, source_target_pairs={{0,15},{1,0},{2,1},{3,2},{4,3},{5,4},{6,5},{7,6},{8,7},{9,8},{10,9... | collective-permute-start | bytes 589832 | tf_op jit(solution)/shard_map/ppermute | solution.py:21
  67.9 6.3 %collective-permute-start.14 = (bf16[24,4096]{1,0:T(8,128)(2,1)S(1)}, bf16[24,4096]{1,0:T(8,128)(2,1)S(1)}, u32[]{:S(2)}, u32[]{:S(2)}) collective-permute-start(bf16[24,4096]{1,0:T(8,128)(2,1)S(1)} %collective-permute-done.12), channel_id=1, source_target_pairs={{0,1},{1,2},{2,3},{3,4},{4,5},{5,6},{6,7},{7,8},{8,9},{9,10},{10,1... | collective-permute-start | bytes 589832 | tf_op jit(solution)/shard_map/ppermute | solution.py:16
  74.9 3.7 %copy-start.7 = (bf16[256,768]{1,0:T(8,128)(2,1)S(1)}, bf16[256,768]{1,0:T(8,128)(2,1)}, u32[]{:S(2)}) copy-start(bf16[256,768]{1,0:T(8,128)(2,1)} %param.11) | copy-start | bytes 1179652
  77.8 0.7 copy-start.8
  78.5 25.3 %copy-start.4 = (f32[1,384]{1,0:T(1,128)S(1)}, f32[1,384]{1,0:T(1,128)}, u32[]{:S(2)}) copy-start(f32[1,384]{1,0:T(1,128)} %constant.139.clone.1) | copy-start | bytes 4612
  78.5 43.1 %copy-start.2 = (bf16[384,96]{0,1:T(8,128)(2,1)S(1)}, bf16[384,96]{0,1:T(8,128)(2,1)}, u32[]{:S(2)}) copy-start(bf16[384,96]{0,1:T(8,128)(2,1)} %param.13) | copy-start | bytes 221188
  78.5 43.1 %copy-start.5 = (f32[96]{0:T(128)S(1)}, f32[96]{0:T(128)}, u32[]{:S(2)}) copy-start(f32[96]{0:T(128)} %param.12) | copy-start | bytes 1156
  80.0 23.6 %all-to-all-start = ((bf16[16,384,48]{1,2,0:T(8,128)(2,1)}), bf16[16,384,48]{1,2,0:T(8,128)(2,1)S(1)}, u32[]{:S(2)}, u32[]{:S(2)}) async-start(bf16[16,384,48]{1,2,0:T(8,128)(2,1)} %bitcast.2), calls=%async_computation | async-start | bytes 1179648 | tf_op jit(solution)/shard_map/all_to_all | solution.py:35
  86.3 77.2 %all-gather.2.cloned.1.call-start = ((), (), s32[]{:S(2)}) async-start(), calls=%async_computation.4 | async-start | bytes 2506752 | tf_op jit(solution)/shard_map/all_gather | solution.py:77
  163.5 2.4 %copy-start.1 = (bf16[1536,768]{1,0:T(8,128)(2,1)S(1)}, bf16[1536,768]{1,0:T(8,128)(2,1)}, u32[]{:S(2)}) copy-start(bf16[1536,768]{1,0:T(8,128)(2,1)} %all-gather.2.cloned.1.call-done) | copy-start | bytes 7077892
  163.5 3.0 %copy-start.9 = (f32[384,256]{1,0:T(8,128)S(1)}, f32[384,256]{1,0:T(8,128)}, u32[]{:S(2)}) copy-start(f32[384,256]{1,0:T(8,128)} %copy-done.8) | copy-start | bytes 1179652
Sparse Core Ops, SparseCore 0:
  123.2 40.2 all-gather.1
